TPU v7x, 32 devices: a whole 2x2x4 slice. The times are simulated.
32 devices in a mesh: groups: 2 (over y), blk: 4 (over z), chan: 4 (over x, core).
Axes of the slice: x: 2, y: 2, z: 4, core: 2. Of those that a mesh axis runs over, the one named last changes fastest.
Arguments:
- fmap1: bfloat16 [128, 256, 128], P(('groups', 'blk'), 'chan'), parts along dimension 0, may hold values from -6 to 6
- fmap2: bfloat16 [128, 256, 128], P(('groups', 'blk'), 'chan'), parts along dimension 0, may hold values from -6 to 6
- windows: int32 [128, 20], P(('groups', 'blk')), parts along dimension 0, may hold values from 0 to 63, as said below
- live: int32 [128], P(('groups', 'blk')), parts along dimension 0, may hold values from 1 to 20, as said below
- cotangent: bfloat16 [128, 20, 128, 128], P(('groups', 'blk')), parts along dimension 0, may hold values from -6 to 6
Outputs:
- grad_one: float32 [128, 256, 128], P(('groups', 'blk'), 'chan'), parts along dimension 0
- grad_two: float32 [128, 256, 128], P(('groups', 'blk'), 'chan'), parts along dimension 0
There are 2 independent parts, one for each index of `groups`. A program takes and returns all parts, laid end to end along the dimension named above; each array names one. Nothing has to cross between parts.
Inputs may be any that keep to these rules, and one draw needn't show every extreme that they name: `windows`: the ids in one row are distinct; they may name blocks anywhere in the frame. Entries at slots live[b] and beyond are padding and carry no weight. `live`: some block uses all 20 slots.
All inputs are finite; a program needn't handle non-finite values.
Results may differ from a plain program's by a relative error of at most 0.0003.
Values may be sent and summed in bfloat16 or wider, within the bound.
A program may use at most 64 MiB of HBM per device.

v0:
```python
import math

import jax
import jax.numpy as jnp
from jax import lax
from jax.sharding import PartitionSpec as P

C = 256


def body(fmap1, fmap2, windows, live, cotangent):
    blocks, channels, site_count = fmap1.shape
    slot_count = windows.shape[1]
    inv_root = 1.0 / math.sqrt(C)
    slot_mask = (jnp.arange(slot_count, dtype=jnp.int32)[None, :] < live[:, None]).astype(
        jnp.float32
    )
    terms = jnp.einsum("bwij,bci->bwcj", cotangent, fmap1, preferred_element_type=jnp.float32)
    terms = terms * (inv_root * slot_mask)[:, :, None, None]
    flat_terms = terms.reshape(blocks * slot_count, channels * site_count)
    flat_ids = windows.reshape(-1)
    piece = lax.all_gather(fmap2, "blk", axis=0, tiled=True)
    piece_rows = piece.shape[0]
    row_ids = jnp.arange(piece_rows, dtype=jnp.int32)
    picker = (flat_ids[:, None] == row_ids[None, :]).astype(jnp.bfloat16)
    fetched = jnp.dot(
        picker, piece.reshape(piece_rows, channels * site_count), preferred_element_type=jnp.float32
    )
    fetched = fetched.astype(jnp.bfloat16).reshape(blocks, slot_count, channels, site_count)
    row_count = blocks * lax.axis_size("blk")
    row_ids = jnp.arange(row_count, dtype=jnp.int32)
    owner_hot = (row_ids[:, None] == flat_ids[None, :]).astype(jnp.float32)
    summed = jnp.dot(
        owner_hot, flat_terms, preferred_element_type=jnp.float32, precision=lax.Precision.HIGHEST
    )
    grad_two = lax.psum_scatter(
        summed.reshape(row_count, channels, site_count), "blk", scatter_dimension=0, tiled=True
    )
    selected = fetched * slot_mask.astype(jnp.bfloat16)[:, :, None, None]
    grad_one = (
        jnp.einsum("bwij,bwcj->bci", cotangent, selected, preferred_element_type=jnp.float32)
        * inv_root
    )
    return (grad_one, grad_two)


def solution(mesh):
    placed = (
        P(("groups", "blk"), "chan", None),
        P(("groups", "blk"), "chan", None),
        P(("groups", "blk"), None),
        P(("groups", "blk")),
        P(("groups", "blk"), None, None, None),
    )
    return jax.shard_map(
        body,
        mesh=mesh,
        in_specs=placed,
        out_specs=(P(("groups", "blk"), "chan", None), P(("groups", "blk"), "chan", None)),
        check_vma=False,
    )
```

profile of v0, /device:TPU:0, one launch (start us, length us, event | category | flops | bytes accessed | tf_op | source)
XLA Modules:
  0.0 94.8 jit_solution(12129404039623603795)
XLA Ops:
  7.2 0.0 copy-start
  7.2 0.0 all-gather.2.cloned.1.call-start
  7.2 0.7 all-gather.2.cloned.1.call-update
  7.9 0.0 reduce-scatter.2.cloned.1.call-start
  8.0 0.8 eq.28
  8.7 0.7 fusion.20
  9.5 0.0 copy-done
  9.5 4.9 %broadcast_multiply_fusion = f32[16,64,20,128]{3,1,2,0:T(8,128)S(1)} fusion(f32[16,20]{1,0:T(8,128)S(1)} %fusion.20, bf16[16,20,128,128]{3,2,1,0:T(8,128)(2,1)} %param.9, bf16[16,64,128]{2,1,0:T(8,128)(2,1)S(1)} %copy-done), kind=kOutput, calls=%fused_computation.5 | convolution fusion | flops 673710080 | bytes 21234944 | tf_op jit(solution)/shard_map/bwij,bci->bwcj/dot_general | solution.py:18
  14.4 0.0 copy-start.1
  14.4 11.9 %fusion = f32[64,64,128]{2,0,1:T(8,128)} fusion(s32[320]{0:T(512)S(1)} %eq.28, f32[40,8,64,128]{3,2,1,0:T(8,128)S(1)} %bitcast.38), kind=kOutput, calls=%fused_computation.2 | convolution fusion | flops 2013286400 | bytes 12584192 | tf_op jit(solution)/shard_map/dot_general | solution.py:33
  26.3 0.0 reduce-scatter.2.cloned.1.call-update
  26.3 0.0 copy-done.1
  26.3 0.1 convert_convert_fusion
  26.4 13.9 %all-gather.2.cloned.1.call-done = bf16[64,64,128]{2,1,0:T(8,128)(2,1)} async-done(((bf16[16,64,128]{2,1,0:T(8,128)(2,1)}), bf16[64,64,128]{2,1,0:T(8,128)(2,1)}) %all-gather.2.cloned.1.call-update) | async-done | bytes 1048592 | tf_op jit(solution)/shard_map/all_gather | solution.py:22
  40.2 2.8 %fusion.6 = bf16[40,8,64,128]{3,1,2,0:T(8,128)(2,1)S(1)} fusion(bf16[8,8,64,128]{3,2,1,0:T(8,128)(2,1)} %bitcast.40, s32[320]{0:T(512)S(1)} %eq.28), kind=kOutput, calls=%fused_computation.9 | convolution fusion | flops 338186240 | bytes 6292736 | tf_op jit(solution)/shard_map/dot_general | solution.py:26
  43.0 1.7 %copy.16 = bf16[40,8,64,128]{3,2,1,0:T(8,128)(2,1)S(1)} copy(bf16[40,8,64,128]{3,1,2,0:T(8,128)(2,1)S(1)} %fusion.6) | data formatting | bytes 10485760
  44.7 8.9 %fusion.10 = f32[16,64,128]{2,1,0:T(8,128)} fusion(bf16[16,20,128,128]{3,2,1,0:T(8,128)(2,1)} %param.9, bf16[16,20,64,128]{3,2,1,0:T(8,128)(2,1)S(1)} %bitcast.39, bf16[16,20]{1,0:T(8,128)(2,1)S(1)} %convert_convert_fusion), kind=kOutput, calls=%fused_computation.11 | convolution fusion | flops 673841152 | bytes 16253568 | tf_op jit(solution)/shard_map/bwij,bwcj->bci/dot_general | solution.py:41
  53.6 32.3 %reduce-scatter.2.cloned.1.call-done = f32[16,64,128]{2,0,1:T(8,128)} async-done(((f32[64,64,128]{2,0,1:T(8,128)}), f32[16,64,128]{2,0,1:T(8,128)}) %reduce-scatter.2.cloned.1.call-update) | async-done | bytes 524304 | tf_op jit(solution)/shard_map/reduce_scatter | solution.py:36
  85.9 2.0 %copy.11 = f32[16,64,128]{2,1,0:T(8,128)} copy(f32[16,64,128]{2,0,1:T(8,128)} %reduce-scatter.2.cloned.1.call-done) | data formatting | bytes 1048576
Async XLA Ops:
  7.2 2.3 %copy-start = (bf16[16,64,128]{2,1,0:T(8,128)(2,1)S(1)}, bf16[16,64,128]{2,1,0:T(8,128)(2,1)}, u32[]{:S(2)}) copy-start(bf16[16,64,128]{2,1,0:T(8,128)(2,1)} %param.5) | copy-start | bytes 786436
  7.2 33.1 %all-gather.2.cloned.1.call-start = ((), (), s32[]{:S(2)}) async-start(), calls=%async_computation.1 | async-start | bytes 1310720 | tf_op jit(solution)/shard_map/all_gather | solution.py:22
  7.9 78.0 %reduce-scatter.2.cloned.1.call-start = ((), (), s32[]{:S(2)}) async-start(), calls=%async_computation.2 | async-start | bytes 2621440 | tf_op jit(solution)/shard_map/reduce_scatter | solution.py:36
  14.4 11.9 %copy-start.1 = (s32[16]{0:T(128)S(1)}, s32[16]{0:T(128)}, u32[]{:S(2)}) copy-start(s32[16]{0:T(128)} %param.8) | copy-start | bytes 196
Sparse Core Ops, SparseCore 0:
  9.6 30.6 all-gather.1
  42.5 43.3 reduce-scatter.1
where the time goes:
time: 95 us; the launch traced here: 94.8 us
  waiting for transfers between devices  46.9 us (49%)
  matrix products  28.5 us (30%)
  between operations  14.1 us (15%)
  local copies, waits for them, and re-layouts  4.45 us (5%)
    reduce_scatter x1, waiting for transfers between devices, body(): lax.psum_scatter(summed.reshape(row_count, channels, site_count), 'blk',...  32.3 us
    all_gather x1, waiting for transfers between devices, body(): piece = lax.all_gather(fmap2, 'blk', axis=0, tiled=True)  13.9 us
    dot_general x1, matrix products, body(): jnp.dot(owner_hot, flat_terms, preferred_element_type=jnp.float32, precis...  11.9 us
    dot_general x1, matrix products, body(): jnp.einsum('bwij,bwcj->bci', cotangent, selected, preferred_element_type=...  8.92 us
    dot_general x1, matrix products, body(): jnp.einsum('bwij,bci->bwcj', cotangent, fmap1, preferred_element_type=jnp...  4.93 us
    unnamed x6, local copies, waits for them, and re-layouts  3.67 us
    dot_general x1, matrix products, body(): jnp.dot(picker, piece.reshape(piece_rows, channels * site_count), preferr...  2.79 us
  transfers between devices with their start and end apart: 2, of which 2 were waited for; matrix products, arithmetic and copies ran while one was open for 33% of the time, Pallas kernels for 0%

commit v1 on v0

v1 whole, which is shorter than its diff:
```python
import functools
import math

import jax
import jax.numpy as jnp
from jax import lax
from jax.experimental import pallas as pl
from jax.experimental.pallas import tpu as pltpu
from jax.sharding import PartitionSpec as P

C = 256
MESH = pl.DeviceIdType.MESH
STEPS = 32767.0
FLOOR = 1e-30


def kernel(n, slots_ref, inverse_ref, f1_hbm, f2_hbm, cot_hbm, one_ref, two_ref,
           f1, cot, terms, held, sums, in_r, in_l, in_scale_r, in_scale_l,
           out_r, out_l, out_scale_r, out_scale_l,
           cot_sem, f1_sem, own_sem, ag_send_r, ag_recv_r, ag_send_l, ag_recv_l,
           rs_send_r, rs_recv_r, rs_send_l, rs_recv_l,
           sc_send_r, sc_recv_r, sc_send_l, sc_recv_l):
    blocks, slots, sites, _ = cot.shape
    channels = f1.shape[1]
    inv_root = 1.0 / math.sqrt(C)
    me = lax.axis_index("blk")
    has_right, has_left = me < n - 1, me > 0
    right, left = {"blk": me + 1}, {"blk": me - 1}

    def cot_copy(b):
        return pltpu.make_async_copy(cot_hbm.at[b], cot.at[b], cot_sem.at[b])

    f1_copy = pltpu.make_async_copy(f1_hbm, f1, f1_sem)
    own_rows = pl.ds(me * blocks, blocks)
    own_copy = pltpu.make_async_copy(f2_hbm, held.at[own_rows], own_sem)
    f1_copy.start()

    @pl.loop(0, blocks)
    def _(b):
        cot_copy(b).start()

    own_copy.start()

    barrier = pltpu.get_barrier_semaphore()

    @pl.when(has_right)
    def _():
        pl.semaphore_signal(barrier, inc=1, device_id=right, device_id_type=MESH)

    @pl.when(has_left)
    def _():
        pl.semaphore_signal(barrier, inc=1, device_id=left, device_id_type=MESH)

    pl.semaphore_wait(barrier, has_right.astype(jnp.int32) + has_left.astype(jnp.int32))

    def gather_copy(src, source, step, send, recv, to):
        rows = pl.ds(source * blocks, blocks)
        return pltpu.make_async_remote_copy(
            src_ref=held.at[rows] if src is None else src,
            dst_ref=held.at[rows],
            send_sem=send.at[step],
            recv_sem=recv.at[step],
            device_id=to,
            device_id_type=MESH,
        )

    @pl.when(has_right)
    def _():
        gather_copy(f2_hbm, me, 0, ag_send_r, ag_recv_r, right).start()

    @pl.when(has_left)
    def _():
        gather_copy(f2_hbm, me, 0, ag_send_l, ag_recv_l, left).start()

    held[n * blocks] = jnp.zeros((channels, sites), held.dtype)
    terms[blocks * slots] = jnp.zeros((channels, sites), jnp.float32)

    f1_copy.wait()
    pair = 2 if slots % 2 == 0 else 1

    @pl.loop(0, blocks)
    def _(b):
        cot_copy(b).wait()
        feat = f1[b]
        for w in range(0, slots, pair):
            tile = jnp.concatenate([cot[b, w + i] for i in range(pair)], axis=1)
            res = jnp.dot(feat, tile, preferred_element_type=jnp.float32)
            for i in range(pair):
                terms[b * slots + w + i] = res[:, i * sites:(i + 1) * sites]

    own_copy.wait()

    def local_sums(chunk):
        @pl.loop(0, blocks)
        def _(k):
            row = chunk * blocks + k
            acc = terms[inverse_ref[row, 0]]
            for b in range(1, blocks):
                acc = acc + terms[inverse_ref[row, b]]
            sums[row] = acc * inv_root

    def chunk_at(j):
        return jnp.where(2 * me < n, n - 1 - j, j)

    def data_copy(d, out, inp, send, recv, to):
        return pltpu.make_async_remote_copy(
            src_ref=out.at[d], dst_ref=inp.at[d], send_sem=send.at[d], recv_sem=recv.at[d],
            device_id=to, device_id_type=MESH)

    def right_copies(d, to):
        return (data_copy(d, out_r, in_r, rs_send_r, rs_recv_r, to),
                data_copy(d, out_scale_r, in_scale_r, sc_send_r, sc_recv_r, to))

    def left_copies(d, to):
        return (data_copy(d, out_l, in_l, rs_send_l, rs_recv_l, to),
                data_copy(d, out_scale_l, in_scale_l, sc_send_l, sc_recv_l, to))

    def encode(d, inp, in_scale, out, out_scale):
        @pl.loop(0, blocks)
        def _(k):
            acc = sums[d * blocks + k]
            if inp is not None:
                acc = acc + inp[d, k].astype(jnp.float32) * in_scale[d, pl.ds(k, 1)]
            most = jnp.maximum(jnp.max(jnp.abs(acc), axis=0, keepdims=True), FLOOR)
            out_scale[d, pl.ds(k, 1)] = most * (1.0 / STEPS)
            coded = jnp.round(acc * (STEPS / most)).astype(jnp.int32)
            out[d, k] = coded.astype(jnp.int16)

    def scatter_step(tau):
        t = tau - me
        d = n - 1 - t

        @pl.when((t >= 0) & (d > me))
        def _():
            @pl.when(has_left)
            def _():
                for c in right_copies(d, left):
                    c.wait_recv()
                encode(d, in_r, in_scale_r, out_r, out_scale_r)

            @pl.when(jnp.logical_not(has_left))
            def _():
                encode(d, None, None, out_r, out_scale_r)

            for c in right_copies(d, right):
                c.start()

        e = tau - (n - 1 - me)

        @pl.when((e >= 0) & (e < me))
        def _():
            @pl.when(has_right)
            def _():
                for c in left_copies(e, right):
                    c.wait_recv()
                encode(e, in_l, in_scale_l, out_l, out_scale_l)

            @pl.when(jnp.logical_not(has_right))
            def _():
                encode(e, None, None, out_l, out_scale_l)

            for c in left_copies(e, left):
                c.start()

    def gather_step(h):
        @pl.when(me - h >= 0)
        def _():
            gather_copy(None, me - h, h - 1, ag_send_r, ag_recv_r, left).wait_recv()

            @pl.when(has_right)
            def _():
                gather_copy(None, me - h, h, ag_send_r, ag_recv_r, right).start()

        @pl.when(me + h <= n - 1)
        def _():
            gather_copy(None, me + h, h - 1, ag_send_l, ag_recv_l, right).wait_recv()

            @pl.when(has_left)
            def _():
                gather_copy(None, me + h, h, ag_send_l, ag_recv_l, left).start()

    def grad_one_block(b):
        picked = jnp.concatenate([held[slots_ref[b, w]] for w in range(slots)], axis=1)
        tile = jnp.concatenate([cot[b, w] for w in range(slots)], axis=1)
        one_ref[b] = lax.dot_general(
            picked, tile, (((1,), (1,)), ((), ())), preferred_element_type=jnp.float32) * inv_root

    complete = jnp.maximum(me, n - 1 - me)
    phases = n - complete

    local_sums(chunk_at(0))
    gather_step(1)
    scatter_step(0)

    @pl.loop(1, n)
    def _(j):
        local_sums(chunk_at(j))

    def ones(h):
        first = (h - complete) * blocks // phases
        last = (h - complete + 1) * blocks // phases

        @pl.when(h >= complete)
        def _():
            @pl.loop(first, last)
            def _(b):
                grad_one_block(b)

    @pl.loop(2, n)
    def _(h):
        gather_step(h)
        scatter_step(h - 1)
        ones(h)

    @pl.when(has_left)
    def _():
        for c in right_copies(me, left):
            c.wait_recv()

        @pl.loop(0, blocks)
        def _(k):
            row = me * blocks + k
            sums[row] = sums[row] + in_r[me, k].astype(jnp.float32) * in_scale_r[me, pl.ds(k, 1)]

    @pl.when(has_right)
    def _():
        for c in left_copies(me, right):
            c.wait_recv()

        @pl.loop(0, blocks)
        def _(k):
            row = me * blocks + k
            sums[row] = sums[row] + in_l[me, k].astype(jnp.float32) * in_scale_l[me, pl.ds(k, 1)]

    two_ref[...] = sums[own_rows]

    @pl.when(has_right)
    def _():
        @pl.loop(0, me + 1)
        def _(h):
            gather_copy(None, me - h, h, ag_send_r, ag_recv_r, right).wait_send()

        @pl.loop(me + 1, n)
        def _(d):
            for c in right_copies(d, right):
                c.wait_send()

    @pl.when(has_left)
    def _():
        @pl.loop(0, n - me)
        def _(h):
            gather_copy(None, me + h, h, ag_send_l, ag_recv_l, left).wait_send()

        @pl.loop(0, me)
        def _(d):
            for c in left_copies(d, left):
                c.wait_send()


def body(fmap1, fmap2, windows, live, cotangent):
    blocks, channels, sites = fmap1.shape
    slots = windows.shape[1]
    n = lax.axis_size("blk")
    rows = n * blocks
    used = jnp.arange(slots, dtype=jnp.int32)[None, :] < live[:, None]
    slot_rows = jnp.where(used, windows, rows)
    pair_ids = jnp.arange(blocks * slots, dtype=jnp.int32).reshape(blocks, slots)
    match = slot_rows[None] == jnp.arange(rows, dtype=jnp.int32)[:, None, None]
    spare = blocks * slots
    inverse = spare + jnp.sum(jnp.where(match, pair_ids[None] - spare, 0), axis=2)

    dma = pltpu.SemaphoreType.DMA
    coded = pltpu.VMEM((n, blocks, channels, sites), jnp.int16)
    scale = pltpu.VMEM((n, blocks, sites), jnp.float32)
    smem = pl.BlockSpec(memory_space=pltpu.SMEM)
    hbm = pl.BlockSpec(memory_space=pl.ANY)
    vmem = pl.BlockSpec(memory_space=pltpu.VMEM)
    shape = jax.ShapeDtypeStruct((blocks, channels, sites), jnp.float32)
    return pl.pallas_call(
        functools.partial(kernel, n),
        out_shape=(shape, shape),
        in_specs=[smem, smem, hbm, hbm, hbm],
        out_specs=(vmem, vmem),
        scratch_shapes=[
            pltpu.VMEM(fmap1.shape, fmap1.dtype),
            pltpu.VMEM(cotangent.shape, cotangent.dtype),
            pltpu.VMEM((spare + 1, channels, sites), jnp.float32),
            pltpu.VMEM((rows + 1, channels, sites), fmap2.dtype),
            pltpu.VMEM((rows, channels, sites), jnp.float32),
            coded, coded, scale, scale, coded, coded, scale, scale,
            dma((blocks,)), dma, dma,
        ] + [dma((n,))] * 12,
        compiler_params=pltpu.CompilerParams(
            collective_id=0, has_side_effects=True, vmem_limit_bytes=56 * 1024 * 1024
        ),
    )(slot_rows, inverse, fmap1, fmap2, cotangent)


def solution(mesh):
    placed = (
        P(("groups", "blk"), "chan", None),
        P(("groups", "blk"), "chan", None),
        P(("groups", "blk"), None),
        P(("groups", "blk")),
        P(("groups", "blk"), None, None, None),
    )
    return jax.shard_map(
        body,
        mesh=mesh,
        in_specs=placed,
        out_specs=(P(("groups", "blk"), "chan", None), P(("groups", "blk"), "chan", None)),
        check_vma=False,
    )
```

time: 95 us -> 40.7 us (0.43)
  waiting for transfers between devices: 46.9 us -> 0 us
  Pallas kernels: 0 us -> 34.2 us
  matrix products: 28.5 us -> 0 us
  between operations: 14.1 us -> 0.65 us
    pallas_call x0 -> x1, Pallas kernels: none -> 34.2 us  [body(): pl.pallas_call(functools.partial(kernel, n), out_shape=(shape, shape), in...]
    reduce_scatter x1 -> x0, waiting for transfers between devices: 32.3 us -> none  [body(): lax.psum_scatter(summed.reshape(row_count, channels, site_count), 'blk',...]
    dot_general x4 -> x0, matrix products: 28.5 us -> none  [the longest x1 11.9 us: body(): jnp.dot(owner_hot, flat_terms, preferred_element_type=jnp.float32, precis...]
    all_gather x1 -> x0, waiting for transfers between devices: 13.9 us -> none  [body(): piece = lax.all_gather(fmap2, 'blk', axis=0, tiled=True)]
    unnamed x6 -> x4, local copies, waits for them, and re-layouts: 3.67 us -> 3.77 us
  transfers between devices with their start and end apart: 2 -> 0, of which waited for: 2 -> 0; matrix products, arithmetic and copies ran while one was open for 33% -> 0% of each run, Pallas kernels for 0% -> 0%
where the time goes in v1:
time: 40.7 us; the launch traced here: 40.3 us
  Pallas kernels  34.2 us (84%)
  local copies, waits for them, and re-layouts  3.94 us (10%)
  other arithmetic  1.56 us (4%)
  between operations  0.65 us (2%)
    pallas_call x1, Pallas kernels, body(): pl.pallas_call(functools.partial(kernel, n), out_shape=(shape, shape), in...  34.2 us
    unnamed x4, local copies, waits for them, and re-layouts  3.77 us

profile of v1, /device:TPU:0, one launch (start us, length us, event | category | flops | bytes accessed | tf_op | source)
XLA Modules:
  0.0 40.3 jit_solution(16771426262852146128)
XLA Ops:
  0.6 0.8 %fusion.slots_ref = s32[16,20]{1,0:T(8,128)S(1)} fusion(s32[16,20]{1,0:T(8,128)} %param.7, s32[16]{0:T(128)} %param.8), kind=kLoop, calls=%fused_computation.5 | loop fusion | flops 640 | bytes 2624 | tf_op jit(solution)/shard_map/jit(_where)/select_n | solution.py:266
  1.4 0.0 copy-start
  1.4 0.1 copy.9
  1.5 0.2 select_reduce_fusion
  1.7 0.1 copy.10
  1.7 0.6 %broadcast_add_fusion.inverse_ref = s32[64,16]{1,0:T(8,128)} fusion(s32[64,16]{1,0:T(8,128)S(1)} %copy.10), kind=kLoop, calls=%fused_computation.2 | loop fusion | flops 1024 | bytes 8192 | tf_op jit(solution)/shard_map/add | solution.py:270
  2.4 0.0 copy-done
  2.4 34.2 %shard_map.68 = (f32[16,64,128]{2,1,0:T(8,128)}, f32[16,64,128]{2,1,0:T(8,128)}) custom-call(s32[16,20]{1,0:T(8,128)} %copy-done, s32[64,16]{1,0:T(8,128)} %broadcast_add_fusion.inverse_ref, bf16[16,64,128]{2,1,0:T(8,128)(2,1)} %f1_hbm.1, bf16[16,64,128]{2,1,0:T(8,128)(2,1)} %f2_hbm.1, bf16[16,20,128,128]{3,2,1,0:T(8,128)(2,1)} %cot_hbm.1), custom_call_target="tpu_custom_call" | custom-call | tf_op jit(solution)/shard_map/pallas_call | solution.py:279
  36.6 1.9 %copy.14 = f32[16,64,128]{2,1,0:T(8,128)} copy(f32[16,64,128]{2,1,0:T(8,128)} %get-tuple-element.4) | data formatting | bytes 1048576
  38.5 1.9 %copy.15 = f32[16,64,128]{2,1,0:T(8,128)} copy(f32[16,64,128]{2,1,0:T(8,128)} %get-tuple-element.5) | data formatting | bytes 1048576
  (1 shorter events, 0.0 us)
Async XLA Ops:
  1.4 1.0 %copy-start = (s32[16,20]{1,0:T(8,128)}, s32[16,20]{1,0:T(8,128)S(1)}, u32[]{:S(2)}) copy-start(s32[16,20]{1,0:T(8,128)S(1)} %fusion.slots_ref) | copy-start | bytes 3844

commit v2 on v1

v2 whole, which is shorter than its diff:
```python
import functools
import math

import jax
import jax.numpy as jnp
from jax import lax
from jax.experimental import pallas as pl
from jax.experimental.pallas import tpu as pltpu
from jax.sharding import PartitionSpec as P

C = 256
MESH = pl.DeviceIdType.MESH
STEPS = 32767.0
FLOOR = 1e-30
CUTS = 2


def kernel(n, slots_ref, inverse_ref, f1_hbm, f2_hbm, cot_hbm, one_ref, two_ref,
           f1, cot, terms, held, sums, in_r, in_l, in_scale_r, in_scale_l,
           out_r, out_l, out_scale_r, out_scale_l,
           cot_sem, f1_sem, own_sem, ag_send_r, ag_recv_r, ag_send_l, ag_recv_l,
           rs_send_r, rs_recv_r, rs_send_l, rs_recv_l,
           sc_send_r, sc_recv_r, sc_send_l, sc_recv_l):
    blocks, slots, sites, _ = cot.shape
    channels = f1.shape[1]
    cuts, sub = in_scale_r.shape[1:3]
    inv_root = 1.0 / math.sqrt(C)
    me = lax.axis_index("blk")
    has_right, has_left = me < n - 1, me > 0
    right, left = {"blk": me + 1}, {"blk": me - 1}

    def cot_copy(b):
        return pltpu.make_async_copy(cot_hbm.at[b], cot.at[b], cot_sem.at[b])

    f1_copy = pltpu.make_async_copy(f1_hbm, f1, f1_sem)
    own_rows = pl.ds(me * blocks, blocks)
    own_copy = pltpu.make_async_copy(f2_hbm, held.at[own_rows], own_sem)
    f1_copy.start()

    @pl.loop(0, blocks)
    def _(b):
        cot_copy(b).start()

    own_copy.start()

    barrier = pltpu.get_barrier_semaphore()

    @pl.when(has_right)
    def _():
        pl.semaphore_signal(barrier, inc=1, device_id=right, device_id_type=MESH)

    @pl.when(has_left)
    def _():
        pl.semaphore_signal(barrier, inc=1, device_id=left, device_id_type=MESH)

    pl.semaphore_wait(barrier, has_right.astype(jnp.int32) + has_left.astype(jnp.int32))

    def gather_copy(src, source, step, q, send, recv, to):
        rows = pl.ds(source * blocks + q * sub, sub)
        return pltpu.make_async_remote_copy(
            src_ref=held.at[rows] if src is None else src.at[pl.ds(q * sub, sub)],
            dst_ref=held.at[rows],
            send_sem=send.at[step * cuts + q],
            recv_sem=recv.at[step * cuts + q],
            device_id=to,
            device_id_type=MESH,
        )

    @pl.loop(0, cuts)
    def _(q):
        @pl.when(has_right)
        def _():
            gather_copy(f2_hbm, me, 0, q, ag_send_r, ag_recv_r, right).start()

        @pl.when(has_left)
        def _():
            gather_copy(f2_hbm, me, 0, q, ag_send_l, ag_recv_l, left).start()

    held[n * blocks] = jnp.zeros((channels, sites), held.dtype)
    terms[blocks * slots] = jnp.zeros((channels, sites), jnp.float32)

    f1_copy.wait()
    pair = 2 if slots % 2 == 0 else 1

    @pl.loop(0, blocks)
    def _(b):
        cot_copy(b).wait()
        feat = f1[b]
        for w in range(0, slots, pair):
            tile = jnp.concatenate([cot[b, w + i] for i in range(pair)], axis=1)
            res = jnp.dot(feat, tile, preferred_element_type=jnp.float32)
            for i in range(pair):
                terms[b * slots + w + i] = res[:, i * sites:(i + 1) * sites]

    own_copy.wait()

    def local_sums(chunk):
        @pl.loop(0, blocks)
        def _(k):
            row = chunk * blocks + k
            acc = terms[inverse_ref[row, 0]]
            for b in range(1, blocks):
                acc = acc + terms[inverse_ref[row, b]]
            sums[row] = acc * inv_root

    def chunk_at(j):
        return jnp.where(2 * me < n, n - 1 - j, j)

    def data_copy(d, q, out, inp, send, recv, to):
        rows = pl.ds(q * sub, sub)
        return pltpu.make_async_remote_copy(
            src_ref=out.at[d, rows], dst_ref=inp.at[d, rows],
            send_sem=send.at[d * cuts + q], recv_sem=recv.at[d * cuts + q],
            device_id=to, device_id_type=MESH)

    def scale_copy(d, q, out, inp, send, recv, to):
        return pltpu.make_async_remote_copy(
            src_ref=out.at[d, q], dst_ref=inp.at[d, q],
            send_sem=send.at[d * cuts + q], recv_sem=recv.at[d * cuts + q],
            device_id=to, device_id_type=MESH)

    def right_copies(d, q, to):
        return (data_copy(d, q, out_r, in_r, rs_send_r, rs_recv_r, to),
                scale_copy(d, q, out_scale_r, in_scale_r, sc_send_r, sc_recv_r, to))

    def left_copies(d, q, to):
        return (data_copy(d, q, out_l, in_l, rs_send_l, rs_recv_l, to),
                scale_copy(d, q, out_scale_l, in_scale_l, sc_send_l, sc_recv_l, to))

    def encode(d, q, inp, in_scale, out, out_scale):
        @pl.loop(0, sub)
        def _(i):
            k = q * sub + i
            acc = sums[d * blocks + k]
            if inp is not None:
                acc = acc + inp[d, k].astype(jnp.float32) * in_scale[d, q, pl.ds(i, 1)]
            most = jnp.maximum(jnp.max(jnp.abs(acc), axis=0, keepdims=True), FLOOR)
            out_scale[d, q, pl.ds(i, 1)] = most * (1.0 / STEPS)
            coded = jnp.round(acc * (STEPS / most)).astype(jnp.int32)
            out[d, k] = coded.astype(jnp.int16)

    def scatter_step(tau, q):
        t = tau - me
        d = n - 1 - t

        @pl.when((t >= 0) & (d > me))
        def _():
            @pl.when(has_left)
            def _():
                for c in right_copies(d, q, left):
                    c.wait_recv()
                encode(d, q, in_r, in_scale_r, out_r, out_scale_r)

            @pl.when(jnp.logical_not(has_left))
            def _():
                encode(d, q, None, None, out_r, out_scale_r)

            for c in right_copies(d, q, right):
                c.start()

        e = tau - (n - 1 - me)

        @pl.when((e >= 0) & (e < me))
        def _():
            @pl.when(has_right)
            def _():
                for c in left_copies(e, q, right):
                    c.wait_recv()
                encode(e, q, in_l, in_scale_l, out_l, out_scale_l)

            @pl.when(jnp.logical_not(has_right))
            def _():
                encode(e, q, None, None, out_l, out_scale_l)

            for c in left_copies(e, q, left):
                c.start()

    def gather_step(h, q):
        @pl.when(me - h >= 0)
        def _():
            gather_copy(None, me - h, h - 1, q, ag_send_r, ag_recv_r, left).wait_recv()

            @pl.when(has_right)
            def _():
                gather_copy(None, me - h, h, q, ag_send_r, ag_recv_r, right).start()

        @pl.when(me + h <= n - 1)
        def _():
            gather_copy(None, me + h, h - 1, q, ag_send_l, ag_recv_l, right).wait_recv()

            @pl.when(has_left)
            def _():
                gather_copy(None, me + h, h, q, ag_send_l, ag_recv_l, left).start()

    def grad_one_block(b):
        picked = jnp.concatenate([held[slots_ref[b, w]] for w in range(slots)], axis=1)
        tile = jnp.concatenate([cot[b, w] for w in range(slots)], axis=1)
        one_ref[b] = lax.dot_general(
            picked, tile, (((1,), (1,)), ((), ())), preferred_element_type=jnp.float32) * inv_root

    ready = jnp.maximum(me, n - 1 - me) * cuts + cuts - 1
    pieces = n * cuts - ready
    local_sums(chunk_at(0))

    @pl.loop(0, cuts)
    def _(q):
        gather_step(1, q)
        scatter_step(0, q)

    @pl.loop(1, n)
    def _(j):
        local_sums(chunk_at(j))

    @pl.loop(2 * cuts, n * cuts)
    def _(u):
        h, q = u // cuts, u % cuts
        gather_step(h, q)
        scatter_step(h - 1, q)

        @pl.when(u >= ready)
        def _():
            @pl.loop((u - ready) * blocks // pieces, (u - ready + 1) * blocks // pieces)
            def _(b):
                grad_one_block(b)

    @pl.loop(0, cuts)
    def _(q):
        @pl.when(has_left)
        def _():
            for c in right_copies(me, q, left):
                c.wait_recv()

        @pl.when(has_right)
        def _():
            for c in left_copies(me, q, right):
                c.wait_recv()

        @pl.loop(0, sub)
        def _(i):
            k = q * sub + i
            two_ref[k] = sums[me * blocks + k]

            @pl.when(has_left)
            def _():
                two_ref[k] += in_r[me, k].astype(jnp.float32) * in_scale_r[me, q, pl.ds(i, 1)]

            @pl.when(has_right)
            def _():
                two_ref[k] += in_l[me, k].astype(jnp.float32) * in_scale_l[me, q, pl.ds(i, 1)]

    @pl.loop(0, cuts)
    def _(q):
        @pl.when(has_right)
        def _():
            @pl.loop(0, me + 1)
            def _(h):
                gather_copy(None, me - h, h, q, ag_send_r, ag_recv_r, right).wait_send()

            @pl.loop(me + 1, n)
            def _(d):
                for c in right_copies(d, q, right):
                    c.wait_send()

        @pl.when(has_left)
        def _():
            @pl.loop(0, n - me)
            def _(h):
                gather_copy(None, me + h, h, q, ag_send_l, ag_recv_l, left).wait_send()

            @pl.loop(0, me)
            def _(d):
                for c in left_copies(d, q, left):
                    c.wait_send()


def finish(one_in, two_in, one_out, two_out):
    one_out[...] = one_in[...]
    two_out[...] = two_in[...]


def body(fmap1, fmap2, windows, live, cotangent):
    blocks, channels, sites = fmap1.shape
    slots = windows.shape[1]
    n = lax.axis_size("blk")
    rows = n * blocks
    used = jnp.arange(slots, dtype=jnp.int32)[None, :] < live[:, None]
    slot_rows = jnp.where(used, windows, rows)
    pair_ids = jnp.arange(blocks * slots, dtype=jnp.int32).reshape(blocks, slots)
    match = slot_rows[None] == jnp.arange(rows, dtype=jnp.int32)[:, None, None]
    spare = blocks * slots
    inverse = spare + jnp.sum(jnp.where(match, pair_ids[None] - spare, 0), axis=2)

    dma = pltpu.SemaphoreType.DMA
    coded = pltpu.VMEM((n, blocks, channels, sites), jnp.int16)
    cuts = math.gcd(CUTS, blocks)
    scale = pltpu.VMEM((n, cuts, blocks // cuts, sites), jnp.float32)
    smem = pl.BlockSpec(memory_space=pltpu.SMEM)
    hbm = pl.BlockSpec(memory_space=pl.ANY)
    vmem = pl.BlockSpec(memory_space=pltpu.VMEM)
    shape = jax.ShapeDtypeStruct((blocks, channels, sites), jnp.float32)
    one, two = pl.pallas_call(
        functools.partial(kernel, n),
        out_shape=(shape, shape),
        in_specs=[smem, smem, hbm, hbm, hbm],
        out_specs=(vmem, vmem),
        scratch_shapes=[
            pltpu.VMEM(fmap1.shape, fmap1.dtype),
            pltpu.VMEM(cotangent.shape, cotangent.dtype),
            pltpu.VMEM((spare + 1, channels, sites), jnp.float32),
            pltpu.VMEM((rows + 1, channels, sites), fmap2.dtype),
            pltpu.VMEM((rows, channels, sites), jnp.float32),
            coded, coded, scale, scale, coded, coded, scale, scale,
            dma((blocks,)), dma, dma,
        ] + [dma((n * cuts,))] * 12,
        compiler_params=pltpu.CompilerParams(
            collective_id=0, has_side_effects=True, vmem_limit_bytes=56 * 1024 * 1024
        ),
    )(slot_rows, inverse, fmap1, fmap2, cotangent)
    cuts_out = math.gcd(4, blocks)
    part = pl.BlockSpec((blocks // cuts_out, channels, sites), lambda i: (i, 0, 0))
    return pl.pallas_call(
        finish,
        out_shape=(shape, shape),
        grid=(cuts_out,),
        in_specs=[part, part],
        out_specs=(part, part),
    )(one, two)


def solution(mesh):
    placed = (
        P(("groups", "blk"), "chan", None),
        P(("groups", "blk"), "chan", None),
        P(("groups", "blk"), None),
        P(("groups", "blk")),
        P(("groups", "blk"), None, None, None),
    )
    return jax.shard_map(
        body,
        mesh=mesh,
        in_specs=placed,
        out_specs=(P(("groups", "blk"), "chan", None), P(("groups", "blk"), "chan", None)),
        check_vma=False,
    )
```

time: 40.7 us -> 39.2 us (0.963)
  local copies, waits for them, and re-layouts: 3.94 us -> 0.17 us
  Pallas kernels: 34.2 us -> 36.5 us
    unnamed x4 -> x2, local copies, waits for them, and re-layouts: 3.77 us -> 0.01 us
    pallas_call x0 -> x1, Pallas kernels: none -> 3.41 us  [body(): pl.pallas_call(finish, out_shape=(shape, shape), grid=(cuts_out,), in_spe...]
    pallas_call x1, Pallas kernels: 34.2 us -> 33.1 us  [body(): pl.pallas_call(functools.partial(kernel, n), out_shape=(shape, shape), in...]
where the time goes in v2:
time: 39.2 us; the launch traced here: 38.9 us
  Pallas kernels  36.5 us (93%)
  other arithmetic  1.56 us (4%)
  between operations  0.65 us (2%)
    pallas_call x1, Pallas kernels, body(): pl.pallas_call(functools.partial(kernel, n), out_shape=(shape, shape), in...  33.1 us
    pallas_call x1, Pallas kernels, body(): pl.pallas_call(finish, out_shape=(shape, shape), grid=(cuts_out,), in_spe...  3.41 us

profile of v2, /device:TPU:0, one launch (start us, length us, event | category | flops | bytes accessed | tf_op | source)
XLA Modules:
  0.0 38.9 jit_solution(13271977950346630431)
XLA Ops:
  0.6 0.8 %fusion.slots_ref = s32[16,20]{1,0:T(8,128)S(1)} fusion(s32[16,20]{1,0:T(8,128)} %param.7, s32[16]{0:T(128)} %param.8), kind=kLoop, calls=%fused_computation.5 | loop fusion | flops 640 | bytes 2624 | tf_op jit(solution)/shard_map/jit(_where)/select_n | solution.py:287
  1.4 0.0 copy-start
  1.4 0.1 copy.9
  1.5 0.2 select_reduce_fusion
  1.7 0.1 copy.10
  1.7 0.6 %broadcast_add_fusion.inverse_ref = s32[64,16]{1,0:T(8,128)} fusion(s32[64,16]{1,0:T(8,128)S(1)} %copy.10), kind=kLoop, calls=%fused_computation.2 | loop fusion | flops 1024 | bytes 8192 | tf_op jit(solution)/shard_map/add | solution.py:291
  2.4 0.0 copy-done
  2.4 33.1 %shard_map.68 = (f32[16,64,128]{2,1,0:T(8,128)}, f32[16,64,128]{2,1,0:T(8,128)}) custom-call(s32[16,20]{1,0:T(8,128)} %copy-done, s32[64,16]{1,0:T(8,128)} %broadcast_add_fusion.inverse_ref, bf16[16,64,128]{2,1,0:T(8,128)(2,1)} %f1_hbm.1, bf16[16,64,128]{2,1,0:T(8,128)(2,1)} %f2_hbm.1, bf16[16,20,128,128]{3,2,1,0:T(8,128)(2,1)} %cot_hbm.1), custom_call_target="tpu_custom_call" | custom-call | tf_op jit(solution)/shard_map/pallas_call | solution.py:301
  35.5 3.4 %shard_map.69 = (f32[16,64,128]{2,1,0:T(8,128)}, f32[16,64,128]{2,1,0:T(8,128)}) custom-call(f32[16,64,128]{2,1,0:T(8,128)} %get-tuple-element.4.one_in, f32[16,64,128]{2,1,0:T(8,128)} %get-tuple-element.5.two_in), custom_call_target="tpu_custom_call" | custom-call | tf_op jit(solution)/shard_map/pallas_call | solution.py:321
  (1 shorter events, 0.0 us)
Async XLA Ops:
  1.4 1.0 %copy-start = (s32[16,20]{1,0:T(8,128)}, s32[16,20]{1,0:T(8,128)S(1)}, u32[]{:S(2)}) copy-start(s32[16,20]{1,0:T(8,128)S(1)} %fusion.slots_ref) | copy-start | bytes 3844

commit v3 on v2

--- a/solution.py
+++ b/solution.py
@@ -273,9 +273,23 @@
                     c.wait_send()
 
 
-def finish(one_in, two_in, one_out, two_out):
-    one_out[...] = one_in[...]
-    two_out[...] = two_in[...]
+def finish(one_in, two_in, one_out, two_out, held, came, left):
+    cuts, rows = came.shape[1], one_in.shape[0] // came.shape[1]
+
+    def copies(i, q):
+        part = pl.ds(q * rows, rows)
+        source, target = ((one_in, one_out), (two_in, two_out))[i]
+        return (pltpu.make_async_copy(source.at[part], held.at[i, part], came.at[i, q]),
+                pltpu.make_async_copy(held.at[i, part], target.at[part], left.at[i, q]))
+
+    order = [(i, q) for q in range(cuts) for i in range(2)]
+    for i, q in order:
+        copies(i, q)[0].start()
+    for i, q in order:
+        copies(i, q)[0].wait()
+        copies(i, q)[1].start()
+    for i, q in order:
+        copies(i, q)[1].wait()
 
 
 def body(fmap1, fmap2, windows, live, cotangent):
@@ -317,13 +331,15 @@
         ),
     )(slot_rows, inverse, fmap1, fmap2, cotangent)
     cuts_out = math.gcd(4, blocks)
-    part = pl.BlockSpec((blocks // cuts_out, channels, sites), lambda i: (i, 0, 0))
     return pl.pallas_call(
         finish,
         out_shape=(shape, shape),
-        grid=(cuts_out,),
-        in_specs=[part, part],
-        out_specs=(part, part),
+        in_specs=[hbm, hbm],
+        out_specs=(hbm, hbm),
+        scratch_shapes=[
+            pltpu.VMEM((2, blocks, channels, sites), jnp.float32),
+            dma((2, cuts_out)), dma((2, cuts_out)),
+        ],
     )(one, two)
 
 

time: 39.2 us -> 37.8 us (0.964)
  Pallas kernels: 36.5 us -> 35.2 us
    pallas_call x1, Pallas kernels: 3.41 us -> 2.09 us  [body(): pl.pallas_call(finish, out_shape=(shape, shape), in_specs=[hbm, hbm], out...]
where the time goes in v3:
time: 37.8 us; the launch traced here: 37.5 us
  Pallas kernels  35.2 us (93%)
  other arithmetic  1.56 us (4%)
  between operations  0.65 us (2%)
    pallas_call x1, Pallas kernels, body(): pl.pallas_call(functools.partial(kernel, n), out_shape=(shape, shape), in...  33.1 us
    pallas_call x1, Pallas kernels, body(): pl.pallas_call(finish, out_shape=(shape, shape), in_specs=[hbm, hbm], out...  2.09 us
    select_n x1, other arithmetic, body(): slot_rows = jnp.where(used, windows, rows)  0.77 us

profile of v3, /device:TPU:0, one launch (start us, length us, event | category | flops | bytes accessed | tf_op | source)
XLA Modules:
  0.0 37.5 jit_solution(1483869293191178674)
XLA Ops:
  0.6 0.8 %fusion.slots_ref = s32[16,20]{1,0:T(8,128)S(1)} fusion(s32[16,20]{1,0:T(8,128)} %param.7, s32[16]{0:T(128)} %param.8), kind=kLoop, calls=%fused_computation.5 | loop fusion | flops 640 | bytes 2624 | tf_op jit(solution)/shard_map/jit(_where)/select_n | solution.py:301
  1.4 0.0 copy-start
  1.4 0.1 copy.9
  1.5 0.2 select_reduce_fusion
  1.7 0.1 copy.10
  1.7 0.6 %broadcast_add_fusion.inverse_ref = s32[64,16]{1,0:T(8,128)} fusion(s32[64,16]{1,0:T(8,128)S(1)} %copy.10), kind=kLoop, calls=%fused_computation.2 | loop fusion | flops 1024 | bytes 8192 | tf_op jit(solution)/shard_map/add | solution.py:305
  2.4 0.0 copy-done
  2.4 33.1 %shard_map.68 = (f32[16,64,128]{2,1,0:T(8,128)}, f32[16,64,128]{2,1,0:T(8,128)}) custom-call(s32[16,20]{1,0:T(8,128)} %copy-done, s32[64,16]{1,0:T(8,128)} %broadcast_add_fusion.inverse_ref, bf16[16,64,128]{2,1,0:T(8,128)(2,1)} %f1_hbm.1, bf16[16,64,128]{2,1,0:T(8,128)(2,1)} %f2_hbm.1, bf16[16,20,128,128]{3,2,1,0:T(8,128)(2,1)} %cot_hbm.1), custom_call_target="tpu_custom_call" | custom-call | tf_op jit(solution)/shard_map/pallas_call | solution.py:315
  35.5 2.1 %shard_map.69 = (f32[16,64,128]{2,1,0:T(8,128)}, f32[16,64,128]{2,1,0:T(8,128)}) custom-call(f32[16,64,128]{2,1,0:T(8,128)} %get-tuple-element.4.one_in, f32[16,64,128]{2,1,0:T(8,128)} %get-tuple-element.5.two_in), custom_call_target="tpu_custom_call" | custom-call | tf_op jit(solution)/shard_map/pallas_call | solution.py:334
  (1 shorter events, 0.0 us)
Async XLA Ops:
  1.4 1.0 %copy-start = (s32[16,20]{1,0:T(8,128)}, s32[16,20]{1,0:T(8,128)S(1)}, u32[]{:S(2)}) copy-start(s32[16,20]{1,0:T(8,128)S(1)} %fusion.slots_ref) | copy-start | bytes 3844

commit v4 on v3

--- a/solution.py
+++ b/solution.py
@@ -120,12 +120,12 @@
             device_id=to, device_id_type=MESH)
 
     def right_copies(d, q, to):
-        return (data_copy(d, q, out_r, in_r, rs_send_r, rs_recv_r, to),
-                scale_copy(d, q, out_scale_r, in_scale_r, sc_send_r, sc_recv_r, to))
+        return (scale_copy(d, q, out_scale_r, in_scale_r, sc_send_r, sc_recv_r, to),
+                data_copy(d, q, out_r, in_r, rs_send_r, rs_recv_r, to))
 
     def left_copies(d, q, to):
-        return (data_copy(d, q, out_l, in_l, rs_send_l, rs_recv_l, to),
-                scale_copy(d, q, out_scale_l, in_scale_l, sc_send_l, sc_recv_l, to))
+        return (scale_copy(d, q, out_scale_l, in_scale_l, sc_send_l, sc_recv_l, to),
+                data_copy(d, q, out_l, in_l, rs_send_l, rs_recv_l, to))
 
     def encode(d, q, inp, in_scale, out, out_scale):
         @pl.loop(0, sub)

time: 37.8 us -> 37.8 us (level)
  no operation moved by 1% of the time
where the time goes in v4:
time: 37.8 us; the launch traced here: 37.5 us
  Pallas kernels  35.2 us (93%)
  other arithmetic  1.56 us (4%)
  between operations  0.65 us (2%)
    pallas_call x1, Pallas kernels, body(): pl.pallas_call(functools.partial(kernel, n), out_shape=(shape, shape), in...  33.1 us
    pallas_call x1, Pallas kernels, body(): pl.pallas_call(finish, out_shape=(shape, shape), in_specs=[hbm, hbm], out...  2.09 us
    select_n x1, other arithmetic, body(): slot_rows = jnp.where(used, windows, rows)  0.77 us

profile of v4, /device:TPU:0, one launch (start us, length us, event | category | flops | bytes accessed | tf_op | source)
XLA Modules:
  0.0 37.5 jit_solution(467834452071608233)
XLA Ops:
  0.6 0.8 %fusion.slots_ref = s32[16,20]{1,0:T(8,128)S(1)} fusion(s32[16,20]{1,0:T(8,128)} %param.7, s32[16]{0:T(128)} %param.8), kind=kLoop, calls=%fused_computation.5 | loop fusion | flops 640 | bytes 2624 | tf_op jit(solution)/shard_map/jit(_where)/select_n | solution.py:301
  1.4 0.0 copy-start
  1.4 0.1 copy.9
  1.5 0.2 select_reduce_fusion
  1.7 0.1 copy.10
  1.7 0.6 %broadcast_add_fusion.inverse_ref = s32[64,16]{1,0:T(8,128)} fusion(s32[64,16]{1,0:T(8,128)S(1)} %copy.10), kind=kLoop, calls=%fused_computation.2 | loop fusion | flops 1024 | bytes 8192 | tf_op jit(solution)/shard_map/add | solution.py:305
  2.4 0.0 copy-done
  2.4 33.1 %shard_map.68 = (f32[16,64,128]{2,1,0:T(8,128)}, f32[16,64,128]{2,1,0:T(8,128)}) custom-call(s32[16,20]{1,0:T(8,128)} %copy-done, s32[64,16]{1,0:T(8,128)} %broadcast_add_fusion.inverse_ref, bf16[16,64,128]{2,1,0:T(8,128)(2,1)} %f1_hbm.1, bf16[16,64,128]{2,1,0:T(8,128)(2,1)} %f2_hbm.1, bf16[16,20,128,128]{3,2,1,0:T(8,128)(2,1)} %cot_hbm.1), custom_call_target="tpu_custom_call" | custom-call | tf_op jit(solution)/shard_map/pallas_call | solution.py:315
  35.4 2.1 %shard_map.69 = (f32[16,64,128]{2,1,0:T(8,128)}, f32[16,64,128]{2,1,0:T(8,128)}) custom-call(f32[16,64,128]{2,1,0:T(8,128)} %get-tuple-element.4.one_in, f32[16,64,128]{2,1,0:T(8,128)} %get-tuple-element.5.two_in), custom_call_target="tpu_custom_call" | custom-call | tf_op jit(solution)/shard_map/pallas_call | solution.py:334
  (1 shorter events, 0.0 us)
Async XLA Ops:
  1.4 1.0 %copy-start = (s32[16,20]{1,0:T(8,128)}, s32[16,20]{1,0:T(8,128)S(1)}, u32[]{:S(2)}) copy-start(s32[16,20]{1,0:T(8,128)S(1)} %fusion.slots_ref) | copy-start | bytes 3844
